TPU v7x, 256 devices: a whole 4x4x8 slice. The times are simulated.
256 devices in a mesh: cfg: 2 (over core), section: 8 (over y, x_hi), patch: 16 (over z, x_lo).
Axes of the slice: x: 4 (x_hi: 2, x_lo: 2; x = x_hi * 2 + x_lo), y: 4, z: 8, core: 2. Of those that a mesh axis runs over, the one named last changes fastest.
Arguments:
- hidden_in: float32 [2, 8, 640, 2432], P('cfg', 'section', 'patch'), may hold values from -12 to 12, as said below
- latent_in: float32 [8, 640, 64], P('section', 'patch'), may hold values from -6 to 6
- kv_cache: bfloat16 [2, 8, 5120, 2, 2048], P('cfg', 'section', None, None, 'patch'), may hold values from -6 to 6
- text_kv: bfloat16 [2, 8, 333, 2, 2048], P('cfg', 'section', None, None, 'patch'), may hold values from -6 to 6
- qkv_weight: bfloat16 [8, 2432, 3, 2048], P('section', None, None, 'patch'), may hold values from -0.125 to 0.125
- out_weight: bfloat16 [8, 2048, 2432], P('section', 'patch'), may hold values from -0.75 to 0.75
- mod_table: float32 [8, 28, 3, 2432], P('section'), may hold values from -4 to 4
- final_mod: float32 [28, 2, 2432], replicated, may hold values from -3 to 3
- final_weight: bfloat16 [2432, 64], replicated, may hold values from -0.125 to 0.125
- embed_weight: bfloat16 [64, 2432], replicated, may hold values from -0.75 to 0.75
- pos_embed: bfloat16 [8, 640, 2432], P(None, 'patch'), may hold values from -6 to 6
- patch_order: int32 [8], replicated, may hold values from 0 to 7, each once
- step_index: int32 [1], replicated, may hold values from 0 to 26
- guidance: int32 [1], replicated, may hold values from 192 to 384
Outputs:
- hidden_out: float32 [2, 8, 640, 2432], P('cfg', 'section', 'patch')
- latent_out: float32 [8, 640, 64], P('section', 'patch')
Inputs may be any that keep to these rules, and one draw needn't show every extreme that they name: `hidden_in`: each row and each feature column is scaled by a factor between e^-1.15 and e^1.15; columns may carry a nonzero mean. `patch_order`: each patch number once.
All inputs are finite; a program needn't handle non-finite values.
Results may differ from a plain program's by a relative error of at most 0.0085.
Values may be sent and summed in bfloat16 or wider, within the bound.
No kernel may reach another device: no remote copies, remote signals or barrier semaphores. Data moves between devices by JAX's collectives and lax.ppermute only.
A program may use at most 128 MiB of HBM per device.

v0:
```python
import jax
import jax.numpy as jnp
from jax import lax
from jax.sharding import PartitionSpec as P

HEAD = 64
NT = 28
TICKS = 2


EPSILON = 1e-06


def partner_2(value, axis, bit):
    mask = 2**bit
    pairs = [(source, source ^ mask) for source in range(lax.axis_size(axis))]
    return lax.ppermute(value, axis, pairs)


def from_behind(value, axis, steps):
    count = lax.axis_size(axis)
    pairs = [(source, (source + steps) % count) for source in range(count)]
    return lax.ppermute(value, axis, pairs)


def sigma_of(time_level):
    frac = 1.0 - time_level.astype(jnp.float32) / NT
    return 3.0 * frac / (1.0 + 2.0 * frac)


def layer_norm(values):
    center = values - jnp.mean(values, axis=-1, keepdims=True)
    return center / jnp.sqrt(jnp.mean(center * center, axis=-1, keepdims=True) + EPSILON)


def head_norm(values):
    shaped = values.reshape(values.shape[0], -1, HEAD)
    scaled = shaped / jnp.sqrt(jnp.mean(shaped * shaped, axis=-1, keepdims=True) + EPSILON)
    return scaled.reshape(values.shape[0], -1).astype(jnp.bfloat16)


def pick_entry(table, wanted):
    slots = jnp.arange(table.shape[0], dtype=jnp.int32)
    return jnp.sum(jnp.where(slots == wanted, table, 0))


def attend(queries, text_keys, text_values, key_rows, value_rows, head_count):

    def one_head(head_id):
        first_col = head_id * HEAD
        query_head = lax.dynamic_slice_in_dim(queries, first_col, HEAD, 1)
        text_key_head = lax.dynamic_slice_in_dim(text_keys, first_col, HEAD, 1)
        text_value_head = lax.dynamic_slice_in_dim(text_values, first_col, HEAD, 1)
        key_head = lax.dynamic_slice_in_dim(key_rows, first_col, HEAD, 1)
        value_head = lax.dynamic_slice_in_dim(value_rows, first_col, HEAD, 1)
        text_exp = jnp.exp(
            jnp.einsum("qd,kd->qk", query_head, text_key_head, preferred_element_type=jnp.float32)
            * HEAD ** (-0.5)
        )
        image_exp = jnp.exp(
            jnp.einsum("qd,kd->qk", query_head, key_head, preferred_element_type=jnp.float32)
            * HEAD ** (-0.5)
        )
        row_total = jnp.sum(text_exp, axis=1, keepdims=True) + jnp.sum(
            image_exp, axis=1, keepdims=True
        )
        summed = jnp.dot(
            text_exp.astype(jnp.bfloat16), text_value_head, preferred_element_type=jnp.float32
        )
        summed = summed + jnp.dot(
            image_exp.astype(jnp.bfloat16), value_head, preferred_element_type=jnp.float32
        )
        return (summed / row_total).astype(jnp.bfloat16)

    stacked = lax.map(one_head, jnp.arange(head_count, dtype=jnp.int32))
    return jnp.transpose(stacked, (1, 0, 2)).reshape(queries.shape[0], head_count * HEAD)


def on_device(
    hidden_in,
    latent_in,
    kv_cache,
    text_kv,
    qkv_weight,
    out_weight,
    mod_table,
    final_mod,
    final_weight,
    embed_weight,
    pos_embed,
    patch_order,
    step_index,
    guidance,
):
    sections = lax.axis_size("section")
    section_id = lax.axis_index("section")
    branch = lax.axis_index("cfg")
    hidden_rows = hidden_in[0, 0]
    latent_rows = latent_in[0]
    kv_store = kv_cache[0, 0]
    text_keys = text_kv[0, 0, :, 0]
    text_values = text_kv[0, 0, :, 1]
    weight_in = qkv_weight[0]
    local_width = weight_in.shape[2]
    weight_flat = weight_in.reshape(weight_in.shape[0], 3 * local_width)
    weight_out = out_weight[0]
    modulation_all = mod_table[0]
    local_rows = hidden_rows.shape[0]
    patch_tokens = local_rows * lax.axis_size("patch")
    head_count = local_width // HEAD
    guide_scale = guidance[0].astype(jnp.float32) / 64.0
    for window_tick in range(TICKS):
        position = sections - 1 + window_tick - section_id
        offset = (position >= sections).astype(jnp.int32)
        patch_id = pick_entry(patch_order, position % sections)
        time_level = step_index[0] + offset
        modulation = lax.dynamic_index_in_dim(modulation_all, time_level, 0, keepdims=False)
        normed = (layer_norm(hidden_rows) * (1.0 + modulation[1]) + modulation[0]).astype(
            jnp.bfloat16
        )
        shard_rows = lax.all_gather(normed, "patch", axis=0, tiled=True)
        mixed_rows = jnp.dot(shard_rows, weight_flat, preferred_element_type=jnp.float32).reshape(
            shard_rows.shape[0], 3, local_width
        )
        projected_all = jnp.stack(
            [
                head_norm(mixed_rows[:, 0]),
                head_norm(mixed_rows[:, 1]),
                mixed_rows[:, 2].astype(jnp.bfloat16),
            ],
            axis=1,
        )
        queries = projected_all[:, 0]
        kv_store = lax.dynamic_update_slice_in_dim(
            kv_store, projected_all[:, 1:], patch_id * patch_tokens, 0
        )
        attended = attend(
            queries, text_keys, text_values, kv_store[:, 0], kv_store[:, 1], head_count
        )
        projected = lax.psum_scatter(
            jnp.dot(attended, weight_out, preferred_element_type=jnp.float32),
            "patch",
            scatter_dimension=0,
            tiled=True,
        )
        updated = hidden_rows + modulation[2] * projected
        final_mods = lax.dynamic_index_in_dim(final_mod, time_level, 0, keepdims=False)
        final_normed = (layer_norm(updated) * (1.0 + final_mods[1]) + final_mods[0]).astype(
            jnp.bfloat16
        )
        velocity = jnp.dot(final_normed, final_weight, preferred_element_type=jnp.float32)
        partner = partner_2(velocity, "cfg", 0)
        conditional = jnp.where(branch == 0, velocity, partner)
        unconditional = jnp.where(branch == 0, partner, velocity)
        guided = unconditional + guide_scale * (conditional - unconditional)
        new_latent = latent_rows + (sigma_of(time_level + 1) - sigma_of(time_level)) * guided
        is_last = section_id == sections - 1
        outgoing_latent = jnp.where(is_last, new_latent, latent_rows)
        position_rows = lax.dynamic_index_in_dim(pos_embed, patch_id, 0, keepdims=False).astype(
            jnp.float32
        )
        outgoing = jnp.where(
            is_last,
            jnp.dot(
                new_latent.astype(jnp.bfloat16), embed_weight, preferred_element_type=jnp.float32
            )
            + position_rows,
            updated,
        )
        hidden_rows, latent_rows = from_behind((outgoing, outgoing_latent), "section", 1)
    return (hidden_rows[None, None], latent_rows[None])


def solution(mesh):
    placed = (
        P("cfg", "section", "patch", None),
        P("section", "patch", None),
        P("cfg", "section", None, None, "patch"),
        P("cfg", "section", None, None, "patch"),
        P("section", None, None, "patch"),
        P("section", "patch", None),
        P("section", None, None, None),
        P(),
        P(),
        P(),
        P(None, "patch", None),
        P(),
        P(),
        P(),
    )
    return jax.shard_map(
        on_device,
        mesh=mesh,
        in_specs=placed,
        out_specs=(P("cfg", "section", "patch", None), P("section", "patch", None)),
        check_vma=False,
    )
```

profile of v0, /device:TPU:1, one launch (start us, length us, event | category | flops | bytes accessed | tf_op | source)
XLA Modules:
  0.0 565.4 jit_solution(10687612494290825928)
XLA Ops:
  9.1 1.4 multiply_reduce_fusion.3
  10.5 1.6 dynamic-slice_reduce_fusion.2
  12.0 1.8 add_convert_fusion.3
  13.9 3.9 copy.31
  17.9 1.9 copy.46
  22.1 74.0 %all-gather.3.cloned.1.call-done = bf16[640,2432]{1,0:T(8,128)(2,1)} async-done(((bf16[40,2432]{1,0:T(8,128)(2,1)}), bf16[640,2432]{1,0:T(8,128)(2,1)}) %all-gather.3.cloned.1.call-update) | async-done | bytes 3112976 | tf_op jit(solution)/shard_map/all_gather | solution.py:121
  96.1 4.2 fusion.50
  101.6 1.9 slice_bitcast_fusion.2
  104.1 15.1 %while.20 = (s32[]{:T(128)}, bf16[2,640,64]{1,2,0:T(8,128)(2,1)}, s32[2]{0:T(128)S(1)}, bf16[640,128]{0,1:T(8,128)(2,1)S(1)}, bf16[333,128]{1,0:T(8,128)(2,1)}, ...) while((s32[]{:T(128)}, bf16[2,640,64]{1,2,0:T(8,128)(2,1)}, ...), condition=%wide.region_8.9_spmd, body=%wide.region_5.8_spmd.sunk | while | flops 907288320 | bytes 32108568 | solution.py:75
  105.4 2.8 fusion.105
  108.2 2.1 fusion.106
  112.9 2.8 fusion.105
  115.7 2.1 fusion.106
  119.2 4.5 fusion.56
  123.9 1.6 fusion.66
  125.5 140.0 %reduce-scatter.9.cloned.1.call-done = f32[40,2432]{1,0:T(8,128)} async-done(((f32[640,2432]{1,0:T(8,128)}), f32[40,2432]{1,0:T(8,128)}) %reduce-scatter.9.cloned.1.call-update) | async-done | bytes 389136
  267.2 1.3 collective-permute-start
  272.5 3.0 collective-permute-start.2
  275.4 11.4 %collective-permute-done.2 = f32[40,2432]{1,0:T(8,128)S(1)} collective-permute-done((f32[40,2432]{1,0:T(8,128)S(1)}, f32[40,2432]{1,0:T(8,128)S(1)}, u32[]{:S(2)}, u32[]{:S(2)}) %collective-permute-start.2) | collective-permute-done | bytes 389152 | tf_op jit(solution)/shard_map/ppermute | solution.py:23
  288.9 76.5 %all-gather.5.cloned.1.call-done = bf16[640,2432]{1,0:T(8,128)(2,1)} async-done(((bf16[40,2432]{1,0:T(8,128)(2,1)}), bf16[640,2432]{1,0:T(8,128)(2,1)}) %all-gather.5.cloned.1.call-update) | async-done | bytes 3112976 | tf_op jit(solution)/shard_map/all_gather | solution.py:121
  365.4 4.2 fusion.48
  370.9 1.9 slice_bitcast_fusion
  374.0 16.3 %while.21 = (s32[]{:T(128)}, bf16[2,640,64]{1,2,0:T(8,128)(2,1)}, s32[2]{0:T(128)}, bf16[640,128]{0,1:T(8,128)(2,1)S(1)}, bf16[333,128]{1,0:T(8,128)(2,1)}, /*in...) while((s32[]{:T(128)}, bf16[2,640,64]{1,2,0:T(8,128)(2,1)}, ...), condition=%wide.region_20.21_spmd, body=%wide.region_17.20_spmd.sunk | while | flops 907288320 | bytes 32108568 | solution.py:75
  375.9 2.8 fusion.113
  378.7 2.1 fusion.114
  384.0 2.8 fusion.113
  386.8 2.1 fusion.114
  390.3 4.5 fusion.54
  395.6 141.0 %reduce-scatter.11.cloned.1.call-done = f32[40,2432]{1,0:T(8,128)} async-done(((f32[640,2432]{1,0:T(8,128)}), f32[40,2432]{1,0:T(8,128)}) %reduce-scatter.11.cloned.1.call-update) | async-done | bytes 389136
  542.7 3.0 collective-permute-start.4
  545.7 1.8 collective-permute-start.5
  547.5 10.0 %collective-permute-done.5 = f32[40,64]{1,0:T(8,128)S(1)} collective-permute-done((f32[40,64]{1,0:T(8,128)S(1)}, f32[40,64]{1,0:T(8,128)S(1)}, u32[]{:S(2)}, u32[]{:S(2)}) %collective-permute-start.5) | collective-permute-done | bytes 10272 | tf_op jit(solution)/shard_map/ppermute | solution.py:23
  (143 shorter events, 26.9 us)
Async XLA Ops:
  7.2 112.1 %copy-start = (bf16[1,128,2432]{2,1,0:T(8,128)(2,1)S(1)}, bf16[1,128,2432]{2,1,0:T(8,128)(2,1)}, u32[]{:S(2)}) copy-start(bf16[1,128,2432]{2,1,0:T(8,128)(2,1)} %param.23) | copy-start | bytes 1867780
  7.2 88.9 %all-gather.3.cloned.1.call-start = ((), (), s32[]{:S(2)}) async-start(), calls=%async_computation.2 | async-start | bytes 3307520 | tf_op jit(solution)/shard_map/all_gather | solution.py:121
  9.1 8.8 %copy-start.4 = (bf16[1,1,5120,2,128]{4,3,2,1,0:T(2,128)(2,1)S(1)}, bf16[1,1,5120,2,128]{4,3,2,1,0:T(2,128)(2,1)}, u32[]{:S(2)}) copy-start(bf16[1,1,5120,2,128]{4,3,2,1,0:T(2,128)(2,1)} %param.20) | copy-start | bytes 7864324
  13.9 251.6 %reduce-scatter.9.cloned.1.call-start = ((), (), s32[]{:S(2)}) async-start(), calls=%async_computation.4 | async-start | bytes 6615040
  17.9 3.3 copy-start.11
  108.2 2.1 copy-start.12
  108.2 2.5 copy-start.9
  115.7 2.1 copy-start.12
  115.7 2.5 copy-start.9
  123.8 141.7 %copy-start.1 = (f32[1,1,40,2432]{3,2,1,0:T(8,128)S(1)}, f32[1,1,40,2432]{3,2,1,0:T(8,128)}, u32[]{:S(2)}) copy-start(f32[1,1,40,2432]{3,2,1,0:T(8,128)} %param.18) | copy-start | bytes 1167364
  123.8 143.1 %copy-start.21 = (bf16[2432,64]{0,1:T(8,128)(2,1)S(1)}, bf16[2432,64]{0,1:T(8,128)(2,1)}, u32[]{:S(2)}) copy-start(bf16[2432,64]{0,1:T(8,128)(2,1)} %param.26) | copy-start | bytes 933892
  123.8 147.5 %copy-start.5 = (bf16[64,2432]{1,0:T(8,128)(2,1)S(1)}, bf16[64,2432]{1,0:T(8,128)(2,1)}, u32[]{:S(2)}) copy-start(bf16[64,2432]{1,0:T(8,128)(2,1)} %param.27) | copy-start | bytes 933892
  123.8 147.5 %copy-start.14 = (f32[1,40,64]{2,1,0:T(8,128)S(1)}, f32[1,40,64]{2,1,0:T(8,128)}, u32[]{:S(2)}) copy-start(f32[1,40,64]{2,1,0:T(8,128)} %param.19) | copy-start | bytes 30724
  123.8 241.5 %all-gather.5.cloned.1.call-start = ((), (), s32[]{:S(2)}) async-start(), calls=%async_computation.3 | async-start | bytes 3307520 | tf_op jit(solution)/shard_map/all_gather | solution.py:121
  265.5 21.7 %copy-start.16 = (f32[2432]{0:T(1024)S(1)}, f32[2432]{0:T(1024)}, u32[]{:S(2)}) copy-start(f32[2432]{0:T(1024)} %get-tuple-element.137) | copy-start | bytes 29188
  265.5 21.7 %copy-start.17 = (f32[2432]{0:T(1024)S(1)}, f32[2432]{0:T(1024)}, u32[]{:S(2)}) copy-start(f32[2432]{0:T(1024)} %get-tuple-element.140) | copy-start | bytes 29188
  267.2 4.1 collective-permute-start
  272.5 14.3 %collective-permute-start.2 = (f32[40,2432]{1,0:T(8,128)S(1)}, f32[40,2432]{1,0:T(8,128)S(1)}, u32[]{:S(2)}, u32[]{:S(2)}) collective-permute-start(f32[40,2432]{1,0:T(8,128)S(1)} %fusion.47), channel_id=1, source_target_pairs={{0,16},{16,32},{32,48},{48,64},{64,80},{80,96},{96,112},{112,0},{1... | collective-permute-start | bytes 1167368 | tf_op jit(solution)/shard_map/ppermute | solution.py:23
  286.8 82.7 %copy-start.2 = (f32[40,2432]{1,0:T(8,128)}, f32[40,2432]{1,0:T(8,128)S(1)}, u32[]{:S(2)}) copy-start(f32[40,2432]{1,0:T(8,128)S(1)} %collective-permute-done.2) | copy-start | bytes 1167364
  288.1 248.5 %reduce-scatter.11.cloned.1.call-start = ((), (), s32[]{:S(2)}) async-start(), calls=%async_computation.5 | async-start | bytes 6615040
  378.7 2.5 copy-start.7
  386.8 2.5 copy-start.7
  394.9 141.7 %copy-start.3 = (f32[40,2432]{1,0:T(8,128)S(1)}, f32[40,2432]{1,0:T(8,128)}, u32[]{:S(2)}) copy-start(f32[40,2432]{1,0:T(8,128)} %copy-done.2) | copy-start | bytes 1167364
  394.9 141.7 %copy-start.15 = (f32[2432]{0:T(1024)S(1)}, f32[2432]{0:T(1024)}, u32[]{:S(2)}) copy-start(f32[2432]{0:T(1024)} %get-tuple-element.136) | copy-start | bytes 29188
  394.9 143.1 %copy-start.18 = (f32[2432]{0:T(1024)S(1)}, f32[2432]{0:T(1024)}, u32[]{:S(2)}) copy-start(f32[2432]{0:T(1024)} %get-tuple-element.142) | copy-start | bytes 29188
  394.9 143.1 %copy-start.19 = (f32[2432]{0:T(1024)S(1)}, f32[2432]{0:T(1024)}, u32[]{:S(2)}) copy-start(f32[2432]{0:T(1024)} %get-tuple-element.144) | copy-start | bytes 29188
  394.9 143.1 %copy-start.22 = (bf16[2432,64]{0,1:T(8,128)(2,1)S(1)}, bf16[2432,64]{0,1:T(8,128)(2,1)}, u32[]{:S(2)}) copy-start(bf16[2432,64]{0,1:T(8,128)(2,1)} %param.26) | copy-start | bytes 933892
  394.9 146.6 %copy-start.6 = (bf16[64,2432]{1,0:T(8,128)(2,1)S(1)}, bf16[64,2432]{1,0:T(8,128)(2,1)}, u32[]{:S(2)}) copy-start(bf16[64,2432]{1,0:T(8,128)(2,1)} %param.27) | copy-start | bytes 933892
  395.0 146.6 %collective-permute-start.1 = (f32[40,64]{1,0:T(8,128)S(1)}, f32[40,64]{1,0:T(8,128)S(1)}, u32[]{:S(2)}, u32[]{:S(2)}) collective-permute-start(f32[40,64]{1,0:T(8,128)S(1)} %bitcast_select_fusion), channel_id=1, source_target_pairs={{0,16},{16,32},{32,48},{48,64},{64,80},{80,96},{96,112},{112,0},{1... | collective-permute-start | bytes 30728 | tf_op jit(solution)/shard_map/ppermute | solution.py:23
  538.3 3.2 collective-permute-start.3
  542.7 14.8 %collective-permute-start.4 = (f32[40,2432]{1,0:T(8,128)S(1)}, f32[40,2432]{1,0:T(8,128)S(1)}, u32[]{:S(2)}, u32[]{:S(2)}) collective-permute-start(f32[40,2432]{1,0:T(8,128)S(1)} %fusion.46), channel_id=1, source_target_pairs={{0,16},{16,32},{32,48},{48,64},{64,80},{80,96},{96,112},{112,0},{1... | collective-permute-start | bytes 1167368 | tf_op jit(solution)/shard_map/ppermute | solution.py:23
  545.7 11.8 %collective-permute-start.5 = (f32[40,64]{1,0:T(8,128)S(1)}, f32[40,64]{1,0:T(8,128)S(1)}, u32[]{:S(2)}, u32[]{:S(2)}) collective-permute-start(f32[40,64]{1,0:T(8,128)S(1)} %broadcast_select_fusion), channel_id=1, source_target_pairs={{0,16},{16,32},{32,48},{48,64},{64,80},{80,96},{96,112},{112,0},{1... | collective-permute-start | bytes 30728 | tf_op jit(solution)/shard_map/ppermute | solution.py:23
  (7 other events, 8.8 us)
Sparse Core Ops, SparseCore 0:
  14.0 82.0 all-gather.2
  123.9 141.5 reduce-scatter.8
  288.2 77.1 all-gather.4
  395.1 141.5 reduce-scatter.10
where the time goes:
time: 566 us; the launch traced here: 565 us
  waiting for transfers between devices  453 us (80%)
  matrix products  42.6 us (8%)
  local copies, waits for them, and re-layouts  22.1 us (4%)
  between operations  20.9 us (4%)
  other arithmetic  12.7 us (2%)
  starting transfers between devices  11.3 us (2%)
    unnamed x6, waiting for transfers between devices  281 us
    all_gather x2, waiting for transfers between devices, on_device(): shard_rows = lax.all_gather(normed, 'patch', axis=0, tiled=True)  150 us
    ppermute x4, waiting for transfers between devices, from_behind(): return lax.ppermute(value, axis, pairs)  21.4 us
  transfers between devices with their start and end apart: 10, of which 6 were waited for; matrix products, arithmetic and copies ran while one was open for 2% of the time, Pallas kernels for 0%

commit v1 on v0

v1 whole, which is shorter than its diff:
```python
import math

import jax
import jax.numpy as jnp
from jax import lax
from jax.experimental import pallas as pl
from jax.experimental.pallas import tpu as pltpu
from jax.sharding import PartitionSpec as P

HEAD = 64
NT = 28
TICKS = 2
EPSILON = 1e-06
BF = jnp.bfloat16
F32 = jnp.float32
VMEM_LIMIT = 48 * 1024 * 1024
Q_SCALE = math.log2(math.e) / math.sqrt(HEAD)
GROUPS = ((0, 1, -1, 2, -2, 3, -3, 4),)
LANES = 128
TEXT_PAD = 384


def params():
    return pltpu.CompilerParams(vmem_limit_bytes=VMEM_LIMIT)


def cost(flops, moved, exps=0):
    return pl.CostEstimate(flops=int(flops), bytes_accessed=int(moved), transcendentals=int(exps))


def sigma_of(time_level):
    frac = 1.0 - time_level.astype(F32) / NT
    return 3.0 * frac / (1.0 + 2.0 * frac)


def normalize(values):
    center = values - jnp.mean(values, axis=-1, keepdims=True)
    return center / jnp.sqrt(jnp.mean(center * center, axis=-1, keepdims=True) + EPSILON)


def norm_rows(hidden, mod_table, level):
    rows, width = hidden.shape

    def kernel(level_ref, hidden_ref, mod_ref, out_ref):
        values = normalize(hidden_ref[...].astype(F32))
        out_ref[...] = (values * (1.0 + mod_ref[0, 1:2]) + mod_ref[0, 0:1]).astype(BF)

    return pl.pallas_call(
        kernel,
        out_shape=jax.ShapeDtypeStruct((rows, width), BF),
        grid_spec=pltpu.PrefetchScalarGridSpec(
            num_scalar_prefetch=1,
            grid=(1,),
            in_specs=[
                pl.BlockSpec((rows, width), lambda i, lv: (0, 0)),
                pl.BlockSpec((1, 3, width), lambda i, lv: (lv[0], 0, 0)),
            ],
            out_specs=pl.BlockSpec((rows, width), lambda i, lv: (0, 0)),
        ),
        compiler_params=params(),
        cost_estimate=cost(10 * rows * width, 6 * rows * width),
        name="norm_rows",
    )(level, hidden, mod_table)


def head_scale(values, factor):
    lane = lax.broadcasted_iota(jnp.int32, values.shape, 1)
    square = values * values
    low = jnp.sum(jnp.where(lane < HEAD, square, 0.0), axis=1, keepdims=True)
    high = jnp.sum(jnp.where(lane < HEAD, 0.0, square), axis=1, keepdims=True)
    total = jnp.where(lane < HEAD, low, high)
    return values * (factor / jnp.sqrt(total * (1.0 / HEAD) + EPSILON))


def project(chunks, weight):
    count = len(chunks)
    rows, width = chunks[0].shape
    total = count * rows
    wide = weight.shape[1]

    def kernel(*refs):
        chunk_refs, (weight_ref, own_ref, other_ref, gathered) = refs[:count], refs[count:]
        for at, ref in enumerate(chunk_refs):
            gathered[at * rows : (at + 1) * rows, :] = ref[...].astype(F32)
        mixed = jnp.dot(gathered[...].astype(BF), weight_ref[...], preferred_element_type=F32)
        for out_ref, first in ((own_ref, 0), (other_ref, 3 * LANES)):
            part = mixed[:, first : first + 3 * LANES]
            out_ref[:, 0:LANES] = head_scale(part[:, 0:LANES], Q_SCALE).astype(BF)
            out_ref[:, LANES : 2 * LANES] = head_scale(part[:, LANES : 2 * LANES], 1.0).astype(BF)
            out_ref[:, 2 * LANES :] = part[:, 2 * LANES :].astype(BF)

    return pl.pallas_call(
        kernel,
        out_shape=[jax.ShapeDtypeStruct((total, 3 * LANES), BF)] * 2,
        in_specs=[pl.BlockSpec(memory_space=pltpu.VMEM)] * (count + 1),
        out_specs=[pl.BlockSpec(memory_space=pltpu.VMEM)] * 2,
        scratch_shapes=[pltpu.VMEM((total, width), F32)],
        compiler_params=params(),
        cost_estimate=cost(2 * total * width * wide, 2 * wide * width + 2 * total * width),
        name="project",
    )(*chunks, weight)


def masked_queries(queries):
    lane = lax.broadcasted_iota(jnp.int32, queries.shape, 1)
    zero = jnp.zeros_like(queries)
    return jnp.where(lane < HEAD, queries, zero), jnp.where(lane < HEAD, zero, queries)


def weigh(query, keys, values):
    scores = lax.dot_general(
        query, keys, (((1,), (1,)), ((), ())), preferred_element_type=F32
    )
    return jnp.dot(jnp.exp2(scores).astype(BF), values, preferred_element_type=F32)


def with_ones(values):
    return jnp.concatenate([values, jnp.ones(values.shape, BF)], axis=1)


def attend_stale(order, own, recv, keys, values, text_keys, text_values, fresh):
    rows = own.shape[0]
    patch_rows = keys.shape[1]
    blocks = order.shape[0]
    extra = len(fresh)

    def kernel(order_ref, own_ref, recv_ref, key_ref, value_ref, text_key_ref, text_value_ref, *rest):
        fresh_refs, acc_ref = rest[:extra], rest[extra]
        step = pl.program_id(0)

        def both(update):
            for place, query_ref in enumerate((own_ref, recv_ref)):
                for head, query in enumerate(masked_queries(query_ref[...])):
                    update(head, pl.ds(place * rows, rows), query)

        @pl.when(step == 0)
        def _():
            def start(head, at, query):
                total = weigh(query, text_key_ref[...], text_value_ref[...])
                if extra:
                    total += weigh(query, fresh_refs[0][...], with_ones(fresh_refs[1][...]))
                acc_ref[head, at] = total

            both(start)

        value_block = with_ones(value_ref[0])

        def more(head, at, query):
            acc_ref[head, at] += weigh(query, key_ref[0], value_block)

        both(more)

    whole = lambda shape: pl.BlockSpec(shape, lambda i, od: (0,) * len(shape))
    block = pl.BlockSpec((1, patch_rows, LANES), lambda i, od: (od[i], 0, 0))
    total_keys = blocks * patch_rows + TEXT_PAD + (patch_rows if extra else 0)
    return pl.pallas_call(
        kernel,
        out_shape=jax.ShapeDtypeStruct((2, 2 * rows, 2 * LANES), F32),
        grid_spec=pltpu.PrefetchScalarGridSpec(
            num_scalar_prefetch=1,
            grid=(blocks,),
            in_specs=[whole((rows, LANES)), whole((rows, LANES)), block, block]
            + [whole(text_keys.shape), whole(text_values.shape)]
            + [whole(array.shape) for array in fresh],
            out_specs=whole((2, 2 * rows, 2 * LANES)),
        ),
        compiler_params=params(),
        cost_estimate=cost(
            4 * 2 * rows * 2 * total_keys * 256, 4 * LANES * total_keys, 4 * rows * total_keys
        ),
        name="attend_stale",
    )(order, own, recv, keys, values, text_keys, text_values, *fresh)


def attend_fresh(place, owns, recvs, accs, chunk):
    count = len(owns)
    sizes = [array.shape[0] for array in owns]
    total = 2 * sum(sizes)
    hops = [k for group in GROUPS for k in group]
    steps = len(hops)

    def kernel(place_ref, *refs):
        own_refs, recv_refs, acc_refs = refs[:count], refs[count : 2 * count], refs[2 * count : 3 * count]
        out_ref, keys_ref, values_ref = refs[3 * count :]
        at = 0
        for own_ref, recv_ref, size in zip(own_refs, recv_refs, sizes):
            for ref in (own_ref, recv_ref):
                keys_ref[at : at + size] = ref[:, LANES : 2 * LANES]
                values_ref[at : at + size] = ref[:, 2 * LANES :]
                at += size
        value_block = with_ones(values_ref[...])
        hop_at = 0
        for own_ref, recv_ref, acc_ref, size in zip(own_refs, recv_refs, acc_refs, sizes):
            for side, ref in enumerate((own_ref, recv_ref)):
                sums = []
                for head, query in enumerate(masked_queries(ref[:, 0:LANES])):
                    sums.append(
                        acc_ref[head, side * size : (side + 1) * size]
                        + weigh(query, keys_ref[...], value_block)
                    )
                lane = lax.broadcasted_iota(jnp.int32, (size, LANES), 1)
                top = jnp.where(lane < HEAD, sums[0][:, :LANES], sums[1][:, :LANES])
                bottom = jnp.where(lane < HEAD, sums[0][:, LANES:], sums[1][:, LANES:])
                result = top / bottom
                for index in range(size // chunk):
                    target = lax.rem(place_ref[0] + steps - hops[hop_at + index], steps)
                    out_ref[target, side] = result[index * chunk : (index + 1) * chunk].astype(BF)
            hop_at += size // chunk

    vmem = pl.BlockSpec(memory_space=pltpu.VMEM)
    return pl.pallas_call(
        kernel,
        out_shape=[
            jax.ShapeDtypeStruct((steps, 2, chunk, LANES), BF),
            jax.ShapeDtypeStruct((total, LANES), BF),
            jax.ShapeDtypeStruct((total, LANES), BF),
        ],
        in_specs=[pl.BlockSpec(memory_space=pltpu.SMEM)] + [vmem] * (3 * count),
        out_specs=[vmem] * 3,
        compiler_params=params(),
        cost_estimate=cost(4 * total * 2 * total * 256, 8 * total * 1024, 2 * total * total),
        name="attend_fresh",
    )(place, *owns, *recvs, *accs)


def out_project(attended, weight):
    sources, _, chunk, _ = attended.shape
    width = weight.shape[1]
    pair = 2

    def kernel(attended_ref, weight_ref, own_ref, other_ref):
        step = pl.program_id(0)
        parts = [
            jnp.concatenate([attended_ref[at, side] for at in range(pair)], axis=1)
            for side in range(2)
        ]
        sums = [jnp.dot(part, weight_ref[...], preferred_element_type=F32) for part in parts]

        @pl.when(step == 0)
        def _():
            own_ref[...] = sums[0]
            other_ref[...] = sums[1]

        @pl.when(step > 0)
        def _():
            own_ref[...] += sums[0]
            other_ref[...] += sums[1]

    return pl.pallas_call(
        kernel,
        out_shape=[jax.ShapeDtypeStruct((chunk, width), F32)] * 2,
        grid=(sources // pair,),
        in_specs=[
            pl.BlockSpec((pair, 2, chunk, LANES), lambda i: (i, 0, 0, 0)),
            pl.BlockSpec((pair * LANES, width), lambda i: (i, 0)),
        ],
        out_specs=[pl.BlockSpec((chunk, width), lambda i: (0, 0))] * 2,
        compiler_params=params(),
        cost_estimate=cost(4 * chunk * sources * LANES * width, 2 * weight.size),
        name="out_project",
    )(attended, weight)


def finish(level, hidden, own, recv, mod_table, final_mod, final_weight):
    rows, width = hidden.shape
    channels = final_weight.shape[1]

    def kernel(level_ref, hidden_ref, own_ref, recv_ref, mod_ref, final_ref, weight_ref, out_ref, vel_ref):
        projected = own_ref[...] + recv_ref[...].astype(F32)
        updated = hidden_ref[...].astype(F32) + mod_ref[0, 2:3] * projected
        out_ref[...] = updated
        values = normalize(updated)
        normed = (values * (1.0 + final_ref[0, 1:2]) + final_ref[0, 0:1]).astype(BF)
        vel_ref[...] = jnp.dot(normed, weight_ref[...], preferred_element_type=F32)

    whole = lambda shape: pl.BlockSpec(shape, lambda i, lv: (0,) * len(shape))
    return pl.pallas_call(
        kernel,
        out_shape=[
            jax.ShapeDtypeStruct((rows, width), F32),
            jax.ShapeDtypeStruct((rows, channels), F32),
        ],
        grid_spec=pltpu.PrefetchScalarGridSpec(
            num_scalar_prefetch=1,
            grid=(1,),
            in_specs=[
                whole((rows, width)),
                whole((rows, width)),
                whole((rows, width)),
                pl.BlockSpec((1, 3, width), lambda i, lv: (lv[0], 0, 0)),
                pl.BlockSpec((1, 2, width), lambda i, lv: (lv[0], 0, 0)),
                whole((width, channels)),
            ],
            out_specs=[whole((rows, width)), whole((rows, channels))],
        ),
        compiler_params=params(),
        cost_estimate=cost(20 * rows * width, 16 * rows * width),
        name="finish",
    )(level, hidden, own, recv, mod_table, final_mod, final_weight)


def embed(patch, flags, scales, velocity, partner, latent, updated, weight, positions):
    rows, width = updated.shape
    channels = latent.shape[1]

    def kernel(patch_ref, flag_ref, scale_ref, vel_ref, partner_ref, latent_ref, updated_ref, weight_ref, pos_ref, out_ref, new_ref):
        first = flag_ref[0] == 0
        last = flag_ref[1] == 1
        velocity, partner = vel_ref[...], partner_ref[...]
        conditional = jnp.where(first, velocity, partner)
        unconditional = jnp.where(first, partner, velocity)
        guided = unconditional + scale_ref[0] * (conditional - unconditional)
        latent = latent_ref[...]
        moved = latent + scale_ref[1] * guided
        new_ref[...] = jnp.where(last, moved, latent)
        embedded = jnp.dot(moved.astype(BF), weight_ref[...], preferred_element_type=F32)
        embedded = embedded + pos_ref[0].astype(F32)
        out_ref[...] = jnp.where(last, embedded, updated_ref[...]).astype(BF)

    whole = lambda shape: pl.BlockSpec(shape, lambda i, pt: (0,) * len(shape))
    smem = pl.BlockSpec(memory_space=pltpu.SMEM)
    return pl.pallas_call(
        kernel,
        out_shape=[
            jax.ShapeDtypeStruct((rows, width), BF),
            jax.ShapeDtypeStruct((rows, channels), F32),
        ],
        grid_spec=pltpu.PrefetchScalarGridSpec(
            num_scalar_prefetch=1,
            grid=(1,),
            in_specs=[
                smem,
                smem,
                whole((rows, channels)),
                whole((rows, channels)),
                whole((rows, channels)),
                whole((rows, width)),
                whole((channels, width)),
                pl.BlockSpec((1, rows, width), lambda i, pt: (pt[0], 0, 0)),
            ],
            out_specs=[whole((rows, width)), whole((rows, channels))],
        ),
        compiler_params=params(),
        cost_estimate=cost(2 * rows * width * channels, 10 * rows * width),
        name="embed",
    )(patch, flags, scales, velocity, partner, latent, updated, weight, positions)


def on_device(
    hidden_in,
    latent_in,
    kv_cache,
    text_kv,
    qkv_weight,
    out_weight,
    mod_table,
    final_mod,
    final_weight,
    embed_weight,
    pos_embed,
    patch_order,
    step_index,
    guidance,
):
    sections = lax.axis_size("section")
    members = lax.axis_size("patch")
    ring = members // 2
    section = lax.axis_index("section")
    branch = lax.axis_index("cfg")
    place = lax.axis_index("patch") // 2

    def along_z(value, hops):
        pairs = [(at, (at + 2 * hops) % members) for at in range(members)]
        return lax.ppermute(value, "patch", pairs)

    def across_x(value):
        return lax.ppermute(value, "patch", [(at, at ^ 1) for at in range(members)])

    def across_cfg(value):
        return lax.ppermute(value, "cfg", [(0, 1), (1, 0)])

    def next_section(value):
        return lax.ppermute(value, "section", [(at, (at + 1) % sections) for at in range(sections)])

    columns = [[2 * z + x for z in range(ring)] for x in range(2)]
    hidden = hidden_in[0, 0]
    latent = latent_in[0]
    chunk = hidden.shape[0]
    patch_rows = chunk * members
    modulation = mod_table[0]
    depth = qkv_weight.shape[1]

    weight_flat = qkv_weight[0].reshape(depth, 3 * LANES)
    weight_both = jnp.concatenate([weight_flat, across_x(weight_flat)], axis=1)
    out_all = lax.all_gather(
        out_weight[0], "patch", axis=0, tiled=True, axis_index_groups=columns
    )
    cache = kv_cache[0, 0]
    keys = cache[:, 0].reshape(-1, patch_rows, LANES)
    values = cache[:, 1].reshape(-1, patch_rows, LANES)
    text = text_kv[0, 0]
    pad = ((0, TEXT_PAD - text.shape[0]), (0, 0))
    text_keys = jnp.pad(text[:, 0], pad)
    text_values = jnp.pad(
        jnp.concatenate([text[:, 1], jnp.ones((text.shape[0], LANES), BF)], axis=1), pad
    )
    guide_scale = guidance[0].astype(F32) / 64.0
    is_last = section == sections - 1
    rolled = jnp.take(patch_order, (jnp.arange(sections) + sections - 1 - section) % sections)
    flags = jnp.stack([branch, is_last.astype(jnp.int32)]).astype(jnp.int32)
    fresh = ()
    for tick in range(TICKS):
        position = sections - 1 + tick - section
        offset = (position >= sections).astype(jnp.int32)
        level = step_index + offset
        normed = norm_rows(hidden, modulation, level)
        owns, recvs, accs = [], [], []
        for group in GROUPS:
            chunks = [along_z(normed, hops) if hops else normed for hops in group]
            own, other = project(chunks, weight_both)
            owns.append(own)
            recvs.append(across_x(other))
        stale = rolled[1 + tick :]
        for own, recv in zip(owns, recvs):
            accs.append(attend_stale(stale, own, recv, keys, values, text_keys, text_values, fresh))
        attended, *fresh = attend_fresh(place[None].astype(jnp.int32), owns, recvs, accs, chunk)
        attended = lax.all_to_all(
            attended, "patch", 0, 0, axis_index_groups=columns
        )
        mine, theirs = out_project(attended, out_all)
        updated, velocity = finish(
            level, hidden, mine, across_x(theirs.astype(BF)), modulation, final_mod, final_weight
        )
        scales = jnp.stack([guide_scale, (sigma_of(level + 1) - sigma_of(level))[0]])
        outgoing, latent = embed(
            rolled[tick][None],
            flags,
            scales,
            velocity,
            across_cfg(velocity),
            latent,
            updated,
            embed_weight,
            pos_embed,
        )
        hidden, latent = next_section(outgoing), next_section(latent)
    return (hidden.astype(F32)[None, None], latent[None])


def solution(mesh):
    placed = (
        P("cfg", "section", "patch", None),
        P("section", "patch", None),
        P("cfg", "section", None, None, "patch"),
        P("cfg", "section", None, None, "patch"),
        P("section", None, None, "patch"),
        P("section", "patch", None),
        P("section", None, None, None),
        P(),
        P(),
        P(),
        P(None, "patch", None),
        P(),
        P(),
        P(),
    )
    return jax.shard_map(
        on_device,
        mesh=mesh,
        in_specs=placed,
        out_specs=(P("cfg", "section", "patch", None), P("section", "patch", None)),
        check_vma=False,
    )
```

time: 566 us -> 244 us (0.43)
  waiting for transfers between devices: 453 us -> 79 us
  starting transfers between devices: 11.3 us -> 64.3 us
  matrix products: 42.6 us -> 0 us
  Pallas kernels: 0 us -> 34.3 us
  blocking collectives: 0 us -> 22 us
  other arithmetic: 12.7 us -> 3.52 us
    unnamed x6 -> x1, waiting for transfers between devices: 281 us -> 0.68 us
    all_gather x2 -> x1, waiting for transfers between devices: 150 us -> 0.01 us  [on_device(): lax.all_gather(out_weight[0], 'patch', axis=0, tiled=True, axis_index_gro...]
    ppermute x6 -> x25, waiting for transfers between devices: 21.4 us -> 71.1 us  [the longest x5 29.5 us: across_x(): return lax.ppermute(value, 'patch', [(at, at ^ 1) for at in range(members)])]
    ppermute x6 -> x25, starting transfers between devices: 10.9 us -> 55.9 us  [the longest x14 32.9 us: along_z(): return lax.ppermute(value, 'patch', pairs)]
    dot_general x24 -> x0, matrix products: 42.6 us -> none  [the longest x4 11.2 us: one_head(): jnp.einsum('qd,kd->qk', query_head, key_head, preferred_element_type=jnp....]
    pallas_call x0 -> x14, Pallas kernels: none -> 34.3 us  [the longest x2 18.5 us: attend_stale(): pl.pallas_call(kernel, out_shape=jax.ShapeDtypeStruct((2, 2 * rows, 2 * L...]
    all_to_all x0 -> x1, blocking collectives: none -> 22 us  [on_device(): lax.all_to_all(attended, 'patch', 0, 0, axis_index_groups=columns)]
    unnamed x38 -> x66, local copies, waits for them, and re-layouts: 7.24 us -> 15.9 us
  transfers between devices with their start and end apart: 10 -> 27, of which waited for: 6 -> 16; matrix products, arithmetic and copies ran while one was open for 2% -> 7% of each run, Pallas kernels for 0% -> 6%
where the time goes in v1:
time: 244 us; the launch traced here: 242 us
  waiting for transfers between devices  79 us (32%)
  starting transfers between devices  64.3 us (26%)
  Pallas kernels  34.3 us (14%)
  local copies, waits for them, and re-layouts  23.4 us (10%)
  blocking collectives  22 us (9%)
  between operations  15.9 us (7%)
  other arithmetic  3.52 us (1%)
    ppermute x14, starting transfers between devices, along_z(): return lax.ppermute(value, 'patch', pairs)  32.9 us
    ppermute x5, waiting for transfers between devices, across_x(): return lax.ppermute(value, 'patch', [(at, at ^ 1) for at in range(members)])  29.5 us
    ppermute x14, waiting for transfers between devices, along_z(): return lax.ppermute(value, 'patch', pairs)  26.6 us
    all_to_all x1, blocking collectives, on_device(): lax.all_to_all(attended, 'patch', 0, 0, axis_index_groups=columns)  22 us
    pallas_call x2, Pallas kernels, attend_stale(): pl.pallas_call(kernel, out_shape=jax.ShapeDtypeStruct((2, 2 * rows, 2 * L...  18.5 us
    unnamed x66, local copies, waits for them, and re-layouts  15.9 us
    ppermute x4, waiting for transfers between devices, next_section(): lax.ppermute(value, 'section', [(at, (at + 1) % sections) for at in range...  13.4 us
    ppermute x2, starting transfers between devices, across_cfg(): return lax.ppermute(value, 'cfg', [(0, 1), (1, 0)])  10.6 us
  transfers between devices with their start and end apart: 27, of which 16 were waited for; matrix products, arithmetic and copies ran while one was open for 7% of the time, Pallas kernels for 6%

profile of v1, /device:TPU:1, one launch (start us, length us, event | category | flops | bytes accessed | tf_op | source)
XLA Modules:
  0.0 242.4 jit_solution(11330684144999110708)
XLA Ops:
  7.9 2.8 %copy.22 = bf16[1,2432,3,128]{1,3,2,0:T(8,128)(2,1)S(1)} copy(bf16[1,2432,3,128]{3,1,2,0:T(8,128)(2,1)} %param.18) | data formatting | bytes 3735552 | tf_op args[4]
  10.7 2.4 copy.24
  18.8 4.0 %collective-permute-start.1 = (bf16[40,2432]{1,0:T(8,128)(2,1)S(1)}, bf16[40,2432]{1,0:T(8,128)(2,1)S(1)}, u32[]{:S(2)}, u32[]{:S(2)}) collective-permute-start(bf16[40,2432]{1,0:T(8,128)(2,1)S(1)} %norm_rows.2.refs_0_), channel_id=1, source_target_pairs={{0,14},{1,15},{2,0},{3,1},{4,2},{5,3},{6,4},{7,5},{8,6},{9,7},{10,... | collective-permute-start | bytes 583688 | tf_op jit(solution)/shard_map/ppermute | solution.py:374
  22.8 3.6 %collective-permute-start.3 = (bf16[40,2432]{1,0:T(8,128)(2,1)S(1)}, bf16[40,2432]{1,0:T(8,128)(2,1)S(1)}, u32[]{:S(2)}, u32[]{:S(2)}) collective-permute-start(bf16[40,2432]{1,0:T(8,128)(2,1)S(1)} %norm_rows.2.refs_0_), channel_id=1, source_target_pairs={{0,12},{1,13},{2,14},{3,15},{4,0},{5,1},{6,2},{7,3},{8,4},{9,5},{1... | collective-permute-start | bytes 583688 | tf_op jit(solution)/shard_map/ppermute | solution.py:374
  26.4 3.6 %copy.35 = bf16[1,1,5120,2,128]{4,2,3,1,0:T(8,128)(2,1)} copy(bf16[1,1,5120,2,128]{4,3,2,1,0:T(2,128)(2,1)} %param.16) | data formatting | bytes 5242880 | tf_op args[2]
  30.7 3.1 %fusion.4 = (bf16[5120,1,128]{2,0,1:T(8,128)(2,1)S(1)}, bf16[5120,1,128]{2,0,1:T(8,128)(2,1)}) fusion(bf16[5120,2,128]{2,0,1:T(8,128)(2,1)} %bitcast.41), kind=kLoop, calls=%fused_computation.26 | loop fusion | bytes 5242880 | tf_op jit(solution)/shard_map/slice | solution.py:400
  35.0 4.2 %collective-permute-start.5 = (bf16[40,2432]{1,0:T(8,128)(2,1)S(1)}, bf16[40,2432]{1,0:T(8,128)(2,1)S(1)}, u32[]{:S(2)}, u32[]{:S(2)}) collective-permute-start(bf16[40,2432]{1,0:T(8,128)(2,1)S(1)} %norm_rows.2.refs_0_), channel_id=1, source_target_pairs={{0,10},{1,11},{2,12},{3,13},{4,14},{5,15},{6,0},{7,1},{8,2},{9,3},... | collective-permute-start | bytes 583688 | tf_op jit(solution)/shard_map/ppermute | solution.py:374
  39.2 15.4 %collective-permute-done.7 = bf16[2432,384]{1,0:T(8,128)(2,1)} collective-permute-done((bf16[2432,384]{1,0:T(8,128)(2,1)}, bf16[2432,384]{1,0:T(8,128)(2,1)}, u32[]{:S(2)}, u32[]{:S(2)}) %collective-permute-start.7) | collective-permute-done | bytes 1867808 | tf_op jit(solution)/shard_map/ppermute | solution.py:377
  54.5 8.2 %collective-permute-start.6 = (bf16[40,2432]{1,0:T(8,128)(2,1)S(1)}, bf16[40,2432]{1,0:T(8,128)(2,1)S(1)}, u32[]{:S(2)}, u32[]{:S(2)}) collective-permute-start(bf16[40,2432]{1,0:T(8,128)(2,1)S(1)} %norm_rows.2.refs_0_), channel_id=1, source_target_pairs={{0,8},{1,9},{2,10},{3,11},{4,12},{5,13},{6,14},{7,15},{8,0},{9,1},... | collective-permute-start | bytes 583688 | tf_op jit(solution)/shard_map/ppermute | solution.py:374
  62.7 2.4 pad_maximum_fusion.refs_8_
  65.2 8.2 %collective-permute-done.6.refs_7_ = bf16[40,2432]{1,0:T(8,128)(2,1)S(1)} collective-permute-done((bf16[40,2432]{1,0:T(8,128)(2,1)S(1)}, bf16[40,2432]{1,0:T(8,128)(2,1)S(1)}, u32[]{:S(2)}, u32[]{:S(2)}) %collective-permute-start.6) | collective-permute-done | bytes 194592 | tf_op jit(solution)/shard_map/ppermute | solution.py:374
  76.5 4.3 %collective-permute-done.8.recv_ref.refs_1_ = bf16[320,384]{1,0:T(8,128)(2,1)S(1)} collective-permute-done((bf16[320,384]{1,0:T(8,128)(2,1)S(1)}, bf16[320,384]{1,0:T(8,128)(2,1)S(1)}, u32[]{:S(2)}, u32[]{:S(2)}) %collective-permute-start.8) | collective-permute-done | bytes 245792 | tf_op jit(solution)/shard_map/ppermute | solution.py:377
  80.8 9.2 %attend_stale.2.refs_2_ = f32[2,640,256]{2,1,0:T(8,128)S(1)} custom-call(s32[7]{0:T(128)S(1)} %slice.26.order_ref, bf16[320,384]{1,0:T(8,128)(2,1)S(1)} %get-tuple-element.22.own_ref.refs_0_, bf16[320,384]{1,0:T(8,128)(2,1)S(1)} %collective-permute-done.8.recv_ref.refs_1_, bf16[8,640,128]{2,1,0:T(8,128)(2,1)S(1)} %bitcast.38, ...), custom_call_target="tpu_custom_call" | custom-call | flops 6375342080 | bytes 2490368 | tf_op jit(solution)/shard_map/attend_stale/pallas_call | solution.py:156
  93.1 8.3 %all-to-all-start = ((bf16[8,2,40,128]{3,2,1,0:T(8,128)(2,1)}), bf16[8,2,40,128]{3,2,1,0:T(8,128)(2,1)S(1)}, u32[]{:S(2)}, u32[]{:S(2)}) async-start(bf16[8,2,40,128]{3,2,1,0:T(8,128)(2,1)} %get-tuple-element.24), calls=%async_computation | async-start | bytes 327680 | tf_op jit(solution)/shard_map/all_to_all | solution.py:427
  102.5 7.3 %all-to-all-done.attended_ref = bf16[8,2,40,128]{3,2,1,0:T(8,128)(2,1)S(1)} async-done(((bf16[8,2,40,128]{3,2,1,0:T(8,128)(2,1)}), bf16[8,2,40,128]{3,2,1,0:T(8,128)(2,1)S(1)}, u32[]{:S(2)}, u32[]{:S(2)}) %all-to-all-start) | async-done | bytes 163872 | tf_op jit(solution)/shard_map/all_to_all | solution.py:427
  109.8 2.4 copy-done.3
  116.0 3.2 %collective-permute-done.9.recv_ref = bf16[40,2432]{1,0:T(8,128)(2,1)S(1)} collective-permute-done((bf16[40,2432]{1,0:T(8,128)(2,1)S(1)}, bf16[40,2432]{1,0:T(8,128)(2,1)S(1)}, u32[]{:S(2)}, u32[]{:S(2)}) %collective-permute-start.9) | collective-permute-done | bytes 194592 | tf_op jit(solution)/shard_map/ppermute | solution.py:377
  119.7 5.8 %collective-permute-start.10 = (f32[40,64]{1,0:T(8,128)S(1)}, f32[40,64]{1,0:T(8,128)S(1)}, u32[]{:S(2)}, u32[]{:S(2)}) collective-permute-start(f32[40,64]{1,0:T(8,128)S(1)} %get-tuple-element.27.vel_ref), channel_id=1, source_target_pairs={{0,128},{128,0},{1,129},{129,1},{2,130},{130,2},{3,131},{131,3},{4... | collective-permute-start | bytes 30728 | tf_op jit(solution)/shard_map/ppermute | solution.py:380
  128.4 2.7 %collective-permute-start.11 = (bf16[40,2432]{1,0:T(8,128)(2,1)}, bf16[40,2432]{1,0:T(8,128)(2,1)S(1)}, u32[]{:S(2)}, u32[]{:S(2)}) collective-permute-start(bf16[40,2432]{1,0:T(8,128)(2,1)} %get-tuple-element.29), channel_id=1, source_target_pairs={{0,16},{16,32},{32,48},{48,64},{64,80},{80,96},{96,112},{112,0},{1... | collective-permute-start | bytes 583688 | tf_op jit(solution)/shard_map/ppermute | solution.py:383
  131.1 7.4 %collective-permute-done.11.hidden_ref = bf16[40,2432]{1,0:T(8,128)(2,1)S(1)} collective-permute-done((bf16[40,2432]{1,0:T(8,128)(2,1)}, bf16[40,2432]{1,0:T(8,128)(2,1)S(1)}, u32[]{:S(2)}, u32[]{:S(2)}) %collective-permute-start.11) | collective-permute-done | bytes 194592 | tf_op jit(solution)/shard_map/ppermute | solution.py:383
  139.1 2.4 collective-permute-start.13
  141.5 3.6 %collective-permute-start.15 = (bf16[40,2432]{1,0:T(8,128)(2,1)S(1)}, bf16[40,2432]{1,0:T(8,128)(2,1)S(1)}, u32[]{:S(2)}, u32[]{:S(2)}) collective-permute-start(bf16[40,2432]{1,0:T(8,128)(2,1)S(1)} %norm_rows.3.refs_0_), channel_id=1, source_target_pairs={{0,12},{1,13},{2,14},{3,15},{4,0},{5,1},{6,2},{7,3},{8,4},{9,5},{1... | collective-permute-start | bytes 583688 | tf_op jit(solution)/shard_map/ppermute | solution.py:374
  145.3 4.3 %collective-permute-start.17 = (bf16[40,2432]{1,0:T(8,128)(2,1)S(1)}, bf16[40,2432]{1,0:T(8,128)(2,1)S(1)}, u32[]{:S(2)}, u32[]{:S(2)}) collective-permute-start(bf16[40,2432]{1,0:T(8,128)(2,1)S(1)} %norm_rows.3.refs_0_), channel_id=1, source_target_pairs={{0,10},{1,11},{2,12},{3,13},{4,14},{5,15},{6,0},{7,1},{8,2},{9,3},... | collective-permute-start | bytes 583688 | tf_op jit(solution)/shard_map/ppermute | solution.py:374
  150.0 4.3 %collective-permute-done.15.refs_4_ = bf16[40,2432]{1,0:T(8,128)(2,1)S(1)} collective-permute-done((bf16[40,2432]{1,0:T(8,128)(2,1)S(1)}, bf16[40,2432]{1,0:T(8,128)(2,1)S(1)}, u32[]{:S(2)}, u32[]{:S(2)}) %collective-permute-start.15) | collective-permute-done | bytes 194592 | tf_op jit(solution)/shard_map/ppermute | solution.py:374
  154.4 13.5 %collective-permute-done.16.refs_5_ = bf16[40,2432]{1,0:T(8,128)(2,1)S(1)} collective-permute-done((bf16[40,2432]{1,0:T(8,128)(2,1)S(1)}, bf16[40,2432]{1,0:T(8,128)(2,1)S(1)}, u32[]{:S(2)}, u32[]{:S(2)}) %collective-permute-start.16) | collective-permute-done | bytes 194592 | tf_op jit(solution)/shard_map/ppermute | solution.py:374
  173.3 3.7 %collective-permute-done.19.recv_ref.refs_1_ = bf16[320,384]{1,0:T(8,128)(2,1)S(1)} collective-permute-done((bf16[320,384]{1,0:T(8,128)(2,1)S(1)}, bf16[320,384]{1,0:T(8,128)(2,1)S(1)}, u32[]{:S(2)}, u32[]{:S(2)}) %collective-permute-start.19) | collective-permute-done | bytes 245792 | tf_op jit(solution)/shard_map/ppermute | solution.py:377
  178.4 9.3 %attend_stale.3.refs_2_ = f32[2,640,256]{2,1,0:T(8,128)S(1)} custom-call(s32[6]{0:T(128)S(1)} %slice.31.order_ref, bf16[320,384]{1,0:T(8,128)(2,1)S(1)} %get-tuple-element.30.own_ref.refs_0_, bf16[320,384]{1,0:T(8,128)(2,1)S(1)} %collective-permute-done.19.recv_ref.refs_1_, bf16[8,640,128]{2,1,0:T(8,128)(2,1)S(1)} %bitcast.39, ...), custom_call_target="tpu_custom_call" | custom-call | flops 6375342080 | bytes 2490368 | tf_op jit(solution)/shard_map/attend_stale/pallas_call | solution.py:156
  189.0 22.0 %all_to_all.10.attended_ref = bf16[8,2,40,128]{3,2,1,0:T(8,128)(2,1)S(1)} all-to-all(bf16[8,2,40,128]{3,2,1,0:T(8,128)(2,1)S(1)} %get-tuple-element.34), channel_id=1, replica_groups={{0,2,4,6,8,10,12,14},{1,3,5,7,9,11,13,15},{16,18,20,22,24,26,28,30},{17..., dimensions={0} | all-to-all | bytes 327680 | tf_op jit(solution)/shard_map/all_to_all | solution.py:427
  211.0 2.3 out_project.3
  215.0 3.0 %collective-permute-done.20.recv_ref = bf16[40,2432]{1,0:T(8,128)(2,1)S(1)} collective-permute-done((bf16[40,2432]{1,0:T(8,128)(2,1)S(1)}, bf16[40,2432]{1,0:T(8,128)(2,1)S(1)}, u32[]{:S(2)}, u32[]{:S(2)}) %collective-permute-start.20) | collective-permute-done | bytes 194592 | tf_op jit(solution)/shard_map/ppermute | solution.py:377
  218.5 4.8 %collective-permute-start.21 = (f32[40,64]{1,0:T(8,128)S(1)}, f32[40,64]{1,0:T(8,128)S(1)}, u32[]{:S(2)}, u32[]{:S(2)}) collective-permute-start(f32[40,64]{1,0:T(8,128)S(1)} %get-tuple-element.37.vel_ref), channel_id=1, source_target_pairs={{0,128},{128,0},{1,129},{129,1},{2,130},{130,2},{3,131},{131,3},{4... | collective-permute-start | bytes 30728 | tf_op jit(solution)/shard_map/ppermute | solution.py:380
  228.2 6.0 %collective-permute-done.24 = f32[40,64]{1,0:T(8,128)S(1)} collective-permute-done((f32[40,64]{1,0:T(8,128)S(1)}, f32[40,64]{1,0:T(8,128)S(1)}, u32[]{:S(2)}, u32[]{:S(2)}) %collective-permute-start.24) | collective-permute-done | bytes 10272 | tf_op jit(solution)/shard_map/ppermute | solution.py:383
  (125 shorter events, 39.0 us)
Async XLA Ops:
  7.2 102.6 %all-gather.3.cloned.1.call-start = ((), (), s32[]{:S(2)}) async-start(), calls=%async_computation.2 | async-start | bytes 5603328 | tf_op jit(solution)/shard_map/all_gather | solution.py:395
  13.1 41.5 %collective-permute-start.7 = (bf16[2432,384]{1,0:T(8,128)(2,1)}, bf16[2432,384]{1,0:T(8,128)(2,1)}, u32[]{:S(2)}, u32[]{:S(2)}) collective-permute-start(bf16[2432,384]{1,0:T(8,128)(2,1)} %copy.24), channel_id=1, source_target_pairs={{0,1},{1,0},{2,3},{3,2},{4,5},{5,4},{6,7},{7,6},{8,9},{9,8},{10,11... | collective-permute-start | bytes 5603336 | tf_op jit(solution)/shard_map/ppermute | solution.py:377
  17.1 17.6 %collective-permute-start = (bf16[40,2432]{1,0:T(8,128)(2,1)S(1)}, bf16[40,2432]{1,0:T(8,128)(2,1)S(1)}, u32[]{:S(2)}, u32[]{:S(2)}) collective-permute-start(bf16[40,2432]{1,0:T(8,128)(2,1)S(1)} %norm_rows.2.refs_0_), channel_id=1, source_target_pairs={{0,2},{1,3},{2,4},{3,5},{4,6},{5,7},{6,8},{7,9},{8,10},{9,11},{10,... | collective-permute-start | bytes 583688 | tf_op jit(solution)/shard_map/ppermute | solution.py:374
  18.8 16.2 %collective-permute-start.1 = (bf16[40,2432]{1,0:T(8,128)(2,1)S(1)}, bf16[40,2432]{1,0:T(8,128)(2,1)S(1)}, u32[]{:S(2)}, u32[]{:S(2)}) collective-permute-start(bf16[40,2432]{1,0:T(8,128)(2,1)S(1)} %norm_rows.2.refs_0_), channel_id=1, source_target_pairs={{0,14},{1,15},{2,0},{3,1},{4,2},{5,3},{6,4},{7,5},{8,6},{9,7},{10,... | collective-permute-start | bytes 583688 | tf_op jit(solution)/shard_map/ppermute | solution.py:374
  22.8 42.4 %collective-permute-start.2 = (bf16[40,2432]{1,0:T(8,128)(2,1)S(1)}, bf16[40,2432]{1,0:T(8,128)(2,1)S(1)}, u32[]{:S(2)}, u32[]{:S(2)}) collective-permute-start(bf16[40,2432]{1,0:T(8,128)(2,1)S(1)} %norm_rows.2.refs_0_), channel_id=1, source_target_pairs={{0,4},{1,5},{2,6},{3,7},{4,8},{5,9},{6,10},{7,11},{8,12},{9,13},{1... | collective-permute-start | bytes 583688 | tf_op jit(solution)/shard_map/ppermute | solution.py:374
  22.8 42.4 %collective-permute-start.3 = (bf16[40,2432]{1,0:T(8,128)(2,1)S(1)}, bf16[40,2432]{1,0:T(8,128)(2,1)S(1)}, u32[]{:S(2)}, u32[]{:S(2)}) collective-permute-start(bf16[40,2432]{1,0:T(8,128)(2,1)S(1)} %norm_rows.2.refs_0_), channel_id=1, source_target_pairs={{0,12},{1,13},{2,14},{3,15},{4,0},{5,1},{6,2},{7,3},{8,4},{9,5},{1... | collective-permute-start | bytes 583688 | tf_op jit(solution)/shard_map/ppermute | solution.py:374
  33.8 47.0 %copy-start.9 = (bf16[5120,1,128]{2,0,1:T(8,128)(2,1)}, bf16[5120,1,128]{2,0,1:T(8,128)(2,1)S(1)}, u32[]{:S(2)}) copy-start(bf16[5120,1,128]{2,0,1:T(8,128)(2,1)S(1)} %get-tuple-element.42) | copy-start | bytes 3932164
  34.7 30.5 %collective-permute-start.4 = (bf16[40,2432]{1,0:T(8,128)(2,1)S(1)}, bf16[40,2432]{1,0:T(8,128)(2,1)S(1)}, u32[]{:S(2)}, u32[]{:S(2)}) collective-permute-start(bf16[40,2432]{1,0:T(8,128)(2,1)S(1)} %norm_rows.2.refs_0_), channel_id=1, source_target_pairs={{0,6},{1,7},{2,8},{3,9},{4,10},{5,11},{6,12},{7,13},{8,14},{9,15},... | collective-permute-start | bytes 583688 | tf_op jit(solution)/shard_map/ppermute | solution.py:374
  35.0 30.2 %collective-permute-start.5 = (bf16[40,2432]{1,0:T(8,128)(2,1)S(1)}, bf16[40,2432]{1,0:T(8,128)(2,1)S(1)}, u32[]{:S(2)}, u32[]{:S(2)}) collective-permute-start(bf16[40,2432]{1,0:T(8,128)(2,1)S(1)} %norm_rows.2.refs_0_), channel_id=1, source_target_pairs={{0,10},{1,11},{2,12},{3,13},{4,14},{5,15},{6,0},{7,1},{8,2},{9,3},... | collective-permute-start | bytes 583688 | tf_op jit(solution)/shard_map/ppermute | solution.py:374
  54.5 18.9 %collective-permute-start.6 = (bf16[40,2432]{1,0:T(8,128)(2,1)S(1)}, bf16[40,2432]{1,0:T(8,128)(2,1)S(1)}, u32[]{:S(2)}, u32[]{:S(2)}) collective-permute-start(bf16[40,2432]{1,0:T(8,128)(2,1)S(1)} %norm_rows.2.refs_0_), channel_id=1, source_target_pairs={{0,8},{1,9},{2,10},{3,11},{4,12},{5,13},{6,14},{7,15},{8,0},{9,1},... | collective-permute-start | bytes 583688 | tf_op jit(solution)/shard_map/ppermute | solution.py:374
  75.1 5.7 %collective-permute-start.8 = (bf16[320,384]{1,0:T(8,128)(2,1)S(1)}, bf16[320,384]{1,0:T(8,128)(2,1)S(1)}, u32[]{:S(2)}, u32[]{:S(2)}) collective-permute-start(bf16[320,384]{1,0:T(8,128)(2,1)S(1)} %get-tuple-element.23), channel_id=1, source_target_pairs={{0,1},{1,0},{2,3},{3,2},{4,5},{5,4},{6,7},{7,6},{8,9},{9,8},{10,11... | collective-permute-start | bytes 737288 | tf_op jit(solution)/shard_map/ppermute | solution.py:377
  93.1 16.7 %all-to-all-start = ((bf16[8,2,40,128]{3,2,1,0:T(8,128)(2,1)}), bf16[8,2,40,128]{3,2,1,0:T(8,128)(2,1)S(1)}, u32[]{:S(2)}, u32[]{:S(2)}) async-start(bf16[8,2,40,128]{3,2,1,0:T(8,128)(2,1)} %get-tuple-element.24), calls=%async_computation | async-start | bytes 327680 | tf_op jit(solution)/shard_map/all_to_all | solution.py:427
  114.6 4.6 %collective-permute-start.9 = (bf16[40,2432]{1,0:T(8,128)(2,1)S(1)}, bf16[40,2432]{1,0:T(8,128)(2,1)S(1)}, u32[]{:S(2)}, u32[]{:S(2)}) collective-permute-start(bf16[40,2432]{1,0:T(8,128)(2,1)S(1)} %convert_element_type.35), channel_id=1, source_target_pairs={{0,1},{1,0},{2,3},{3,2},{4,5},{5,4},{6,7},{7,6},{8,9},{9,8},{10,11... | collective-permute-start | bytes 583688 | tf_op jit(solution)/shard_map/ppermute | solution.py:377
  119.7 6.6 %collective-permute-start.10 = (f32[40,64]{1,0:T(8,128)S(1)}, f32[40,64]{1,0:T(8,128)S(1)}, u32[]{:S(2)}, u32[]{:S(2)}) collective-permute-start(f32[40,64]{1,0:T(8,128)S(1)} %get-tuple-element.27.vel_ref), channel_id=1, source_target_pairs={{0,128},{128,0},{1,129},{129,1},{2,130},{130,2},{3,131},{131,3},{4... | collective-permute-start | bytes 30728 | tf_op jit(solution)/shard_map/ppermute | solution.py:380
  128.4 10.1 %collective-permute-start.11 = (bf16[40,2432]{1,0:T(8,128)(2,1)}, bf16[40,2432]{1,0:T(8,128)(2,1)S(1)}, u32[]{:S(2)}, u32[]{:S(2)}) collective-permute-start(bf16[40,2432]{1,0:T(8,128)(2,1)} %get-tuple-element.29), channel_id=1, source_target_pairs={{0,16},{16,32},{32,48},{48,64},{64,80},{80,96},{96,112},{112,0},{1... | collective-permute-start | bytes 583688 | tf_op jit(solution)/shard_map/ppermute | solution.py:383
  138.5 38.5 %copy-start.10 = (bf16[5120,1,128]{2,0,1:T(8,128)(2,1)S(1)}, bf16[5120,1,128]{2,0,1:T(8,128)(2,1)}, u32[]{:S(2)}) copy-start(bf16[5120,1,128]{2,0,1:T(8,128)(2,1)} %copy-done.9) | copy-start | bytes 3932164
  138.5 38.5 %copy-start.18 = (bf16[384,128]{1,0:T(8,128)(2,1)S(1)}, bf16[384,128]{1,0:T(8,128)(2,1)}, u32[]{:S(2)}) copy-start(bf16[384,128]{1,0:T(8,128)(2,1)} %copy-done.17) | copy-start | bytes 294916
  138.8 6.5 %collective-permute-start.12 = (bf16[40,2432]{1,0:T(8,128)(2,1)S(1)}, bf16[40,2432]{1,0:T(8,128)(2,1)S(1)}, u32[]{:S(2)}, u32[]{:S(2)}) collective-permute-start(bf16[40,2432]{1,0:T(8,128)(2,1)S(1)} %norm_rows.3.refs_0_), channel_id=1, source_target_pairs={{0,2},{1,3},{2,4},{3,5},{4,6},{5,7},{6,8},{7,9},{8,10},{9,11},{10,... | collective-permute-start | bytes 583688 | tf_op jit(solution)/shard_map/ppermute | solution.py:374
  139.1 10.4 %collective-permute-start.13 = (bf16[40,2432]{1,0:T(8,128)(2,1)S(1)}, bf16[40,2432]{1,0:T(8,128)(2,1)S(1)}, u32[]{:S(2)}, u32[]{:S(2)}) collective-permute-start(bf16[40,2432]{1,0:T(8,128)(2,1)S(1)} %norm_rows.3.refs_0_), channel_id=1, source_target_pairs={{0,14},{1,15},{2,0},{3,1},{4,2},{5,3},{6,4},{7,5},{8,6},{9,7},{10,... | collective-permute-start | bytes 583688 | tf_op jit(solution)/shard_map/ppermute | solution.py:374
  141.5 8.5 %collective-permute-start.14 = (bf16[40,2432]{1,0:T(8,128)(2,1)S(1)}, bf16[40,2432]{1,0:T(8,128)(2,1)S(1)}, u32[]{:S(2)}, u32[]{:S(2)}) collective-permute-start(bf16[40,2432]{1,0:T(8,128)(2,1)S(1)} %norm_rows.3.refs_0_), channel_id=1, source_target_pairs={{0,4},{1,5},{2,6},{3,7},{4,8},{5,9},{6,10},{7,11},{8,12},{9,13},{1... | collective-permute-start | bytes 583688 | tf_op jit(solution)/shard_map/ppermute | solution.py:374
  141.5 12.9 %collective-permute-start.15 = (bf16[40,2432]{1,0:T(8,128)(2,1)S(1)}, bf16[40,2432]{1,0:T(8,128)(2,1)S(1)}, u32[]{:S(2)}, u32[]{:S(2)}) collective-permute-start(bf16[40,2432]{1,0:T(8,128)(2,1)S(1)} %norm_rows.3.refs_0_), channel_id=1, source_target_pairs={{0,12},{1,13},{2,14},{3,15},{4,0},{5,1},{6,2},{7,3},{8,4},{9,5},{1... | collective-permute-start | bytes 583688 | tf_op jit(solution)/shard_map/ppermute | solution.py:374
  145.1 22.8 %collective-permute-start.16 = (bf16[40,2432]{1,0:T(8,128)(2,1)S(1)}, bf16[40,2432]{1,0:T(8,128)(2,1)S(1)}, u32[]{:S(2)}, u32[]{:S(2)}) collective-permute-start(bf16[40,2432]{1,0:T(8,128)(2,1)S(1)} %norm_rows.3.refs_0_), channel_id=1, source_target_pairs={{0,6},{1,7},{2,8},{3,9},{4,10},{5,11},{6,12},{7,13},{8,14},{9,15},... | collective-permute-start | bytes 583688 | tf_op jit(solution)/shard_map/ppermute | solution.py:374
  145.3 22.6 %collective-permute-start.17 = (bf16[40,2432]{1,0:T(8,128)(2,1)S(1)}, bf16[40,2432]{1,0:T(8,128)(2,1)S(1)}, u32[]{:S(2)}, u32[]{:S(2)}) collective-permute-start(bf16[40,2432]{1,0:T(8,128)(2,1)S(1)} %norm_rows.3.refs_0_), channel_id=1, source_target_pairs={{0,10},{1,11},{2,12},{3,13},{4,14},{5,15},{6,0},{7,1},{8,2},{9,3},... | collective-permute-start | bytes 583688 | tf_op jit(solution)/shard_map/ppermute | solution.py:374
  149.6 18.5 %collective-permute-start.18 = (bf16[40,2432]{1,0:T(8,128)(2,1)S(1)}, bf16[40,2432]{1,0:T(8,128)(2,1)S(1)}, u32[]{:S(2)}, u32[]{:S(2)}) collective-permute-start(bf16[40,2432]{1,0:T(8,128)(2,1)S(1)} %norm_rows.3.refs_0_), channel_id=1, source_target_pairs={{0,8},{1,9},{2,10},{3,11},{4,12},{5,13},{6,14},{7,15},{8,0},{9,1},... | collective-permute-start | bytes 583688 | tf_op jit(solution)/shard_map/ppermute | solution.py:374
  171.8 5.1 %collective-permute-start.19 = (bf16[320,384]{1,0:T(8,128)(2,1)S(1)}, bf16[320,384]{1,0:T(8,128)(2,1)S(1)}, u32[]{:S(2)}, u32[]{:S(2)}) collective-permute-start(bf16[320,384]{1,0:T(8,128)(2,1)S(1)} %get-tuple-element.31), channel_id=1, source_target_pairs={{0,1},{1,0},{2,3},{3,2},{4,5},{5,4},{6,7},{7,6},{8,9},{9,8},{10,11... | collective-permute-start | bytes 737288 | tf_op jit(solution)/shard_map/ppermute | solution.py:377
  176.9 34.1 %slice-start = ((s8[4980736]{0:T(1024)(128)(4,1)}), s8[4194304]{0:T(1024)(128)(4,1)S(1)}, s32[]{:S(2)}) async-start(s8[4980736]{0:T(1024)(128)(4,1)} %bitcast.31), calls=%async_computation.3 | async-start | bytes 8388608
  178.4 32.6 %slice-start.1 = ((s8[4980736]{0:T(1024)(128)(4,1)}), s8[786432]{0:T(1024)(128)(4,1)S(1)}, s32[]{:S(2)}) async-start(s8[4980736]{0:T(1024)(128)(4,1)} %bitcast.31), calls=%async_computation.4 | async-start | bytes 1572864
  213.4 4.6 %collective-permute-start.20 = (bf16[40,2432]{1,0:T(8,128)(2,1)S(1)}, bf16[40,2432]{1,0:T(8,128)(2,1)S(1)}, u32[]{:S(2)}, u32[]{:S(2)}) collective-permute-start(bf16[40,2432]{1,0:T(8,128)(2,1)S(1)} %convert_element_type.36), channel_id=1, source_target_pairs={{0,1},{1,0},{2,3},{3,2},{4,5},{5,4},{6,7},{7,6},{8,9},{9,8},{10,11... | collective-permute-start | bytes 583688 | tf_op jit(solution)/shard_map/ppermute | solution.py:377
  214.6 8.8 %collective-permute-start.22 = (f32[40,64]{1,0:T(8,128)S(1)}, f32[40,64]{1,0:T(8,128)S(1)}, u32[]{:S(2)}, u32[]{:S(2)}) collective-permute-start(f32[40,64]{1,0:T(8,128)S(1)} %get-tuple-element.38), channel_id=1, source_target_pairs={{0,16},{16,32},{32,48},{48,64},{64,80},{80,96},{96,112},{112,0},{1... | collective-permute-start | bytes 30728 | tf_op jit(solution)/shard_map/ppermute | solution.py:383
  218.5 5.7 %collective-permute-start.21 = (f32[40,64]{1,0:T(8,128)S(1)}, f32[40,64]{1,0:T(8,128)S(1)}, u32[]{:S(2)}, u32[]{:S(2)}) collective-permute-start(f32[40,64]{1,0:T(8,128)S(1)} %get-tuple-element.37.vel_ref), channel_id=1, source_target_pairs={{0,128},{128,0},{1,129},{129,1},{2,130},{130,2},{3,131},{131,3},{4... | collective-permute-start | bytes 30728 | tf_op jit(solution)/shard_map/ppermute | solution.py:380
  225.5 8.7 %collective-permute-start.23 = (bf16[40,2432]{1,0:T(8,128)(2,1)S(1)}, bf16[40,2432]{1,0:T(8,128)(2,1)S(1)}, u32[]{:S(2)}, u32[]{:S(2)}) collective-permute-start(bf16[40,2432]{1,0:T(8,128)(2,1)S(1)} %get-tuple-element.40), channel_id=1, source_target_pairs={{0,16},{16,32},{32,48},{48,64},{64,80},{80,96},{96,112},{112,0},{1... | collective-permute-start | bytes 583688 | tf_op jit(solution)/shard_map/ppermute | solution.py:383
  226.0 8.2 %collective-permute-start.24 = (f32[40,64]{1,0:T(8,128)S(1)}, f32[40,64]{1,0:T(8,128)S(1)}, u32[]{:S(2)}, u32[]{:S(2)}) collective-permute-start(f32[40,64]{1,0:T(8,128)S(1)} %get-tuple-element.41), channel_id=1, source_target_pairs={{0,16},{16,32},{32,48},{48,64},{64,80},{80,96},{96,112},{112,0},{1... | collective-permute-start | bytes 30728 | tf_op jit(solution)/shard_map/ppermute | solution.py:383
  (25 other events, 202.8 us)
Sparse Core Ops, SparseCore 0:
  9.8 94.7 all-gather.2
